TPU v7x, 512 devices: a whole 4x4x16 slice. The times are simulated.
512 devices in a mesh: dom: 128 (over x, z, core), tile: 4 (over y).
Axes of the slice: x: 4, y: 4, z: 16, core: 2. Of those that a mesh axis runs over, the one named last changes fastest.
Arguments:
- pumping: float32 [8192, 4096], P(('dom', 'tile')), may hold values from -36 to 36
- coupling: float32 [8192, 4096], P(('dom', 'tile')), may hold values from -0.75 to 0.75
- storage: float32 [8192, 64], P(('dom', 'tile')), may hold values from 0.2 to 2
- tile_order: int32 [512, 1024], P(('dom', 'tile')), may hold values from 0 to 1023, each once within a row
- kriging: bfloat16 [8192, 1024], P(('dom', 'tile')), may hold values from -0.75 to 0.75
Outputs:
- sensitivity: float32 [8192, 64], P(('dom', 'tile'))
- residual_gram: float32 [64, 64], replicated
All inputs are finite; a program needn't handle non-finite values.
Results may differ from a plain program's by a relative error of at most 0.00105.
Values may be sent and summed in bfloat16 or wider, within the bound.
No kernel may reach another device: no remote copies, remote signals or barrier semaphores. Data moves between devices by JAX's collectives and lax.ppermute only.
A program may use at most 64 MiB of HBM per device.

v0:
```python
import jax
import jax.numpy as jnp
from jax import lax
from jax.sharding import PartitionSpec as P

FX = 8
FY = 2
ITERS = 2
PRECISE = lax.Precision.HIGHEST


def padded_2(shard, sides, width):
    for axis, dim in sides:
        devices, length = (lax.axis_size(axis), shard.shape[dim])
        up = [(i, (i + 1) % devices) for i in range(devices - 1)]
        down = [(j, i) for i, j in up]
        last = lax.slice_in_dim(shard, length - width, length, axis=dim)
        initial = lax.slice_in_dim(shard, 0, width, axis=dim)
        before = lax.ppermute(last, axis, up)
        after = lax.ppermute(initial, axis, down)
        shard = jnp.concatenate([before, shard, after], axis=dim)
    return shard


def symmetric(matrix):
    return 0.5 * (matrix + matrix.T)


def gram_matrix(left, right):
    return jnp.einsum("brc,bsc->rs", left, right, precision=PRECISE)


def mix_rows(weights, values):
    return jnp.einsum("rs,brc->bsc", weights, values, precision=PRECISE)


def solve_definite(matrix, target):
    factor = jnp.linalg.cholesky(matrix)
    lower_part = lax.linalg.triangular_solve(factor, target, left_side=True, lower=True)
    return lax.linalg.triangular_solve(
        factor, lower_part, left_side=True, lower=True, transpose_a=True
    )


def total_squares(residual):
    return symmetric(lax.psum(gram_matrix(residual, residual), ("dom", "tile")))


def apply_operator(values, matrices, capacity):
    spread = jnp.einsum("brc,bce->bre", values, matrices, precision=PRECISE)
    patch_grid = spread.reshape(FX, FY, -1)
    padded = padded_2(patch_grid.astype(jnp.bfloat16), (("dom", 0), ("tile", 1)), 1).astype(
        patch_grid.dtype
    )
    beside = padded[:-2, 1:-1] + padded[2:, 1:-1] + padded[1:-1, :-2] + padded[1:-1, 2:]
    pulled = (4.0 * patch_grid - beside).reshape(values.shape)
    return capacity[:, None, :] * values + jnp.einsum(
        "bre,bce->brc", pulled, matrices, precision=PRECISE
    )


def shards(pumping, coupling, storage, tile_order, kriging):
    blocks = storage.shape[0]
    width_block = storage.shape[1]
    test_count = pumping.shape[1] // width_block
    groups = lax.axis_size("dom")
    matrices = coupling.reshape(blocks, width_block, width_block)
    residual = pumping.reshape(blocks, test_count, width_block)
    direction = residual
    solution = jnp.zeros_like(residual)
    residual_gram = total_squares(residual)
    for iteration in range(ITERS):
        applied = apply_operator(direction, matrices, storage)
        curvature = symmetric(lax.psum(gram_matrix(direction, applied), ("dom", "tile")))
        step_size = solve_definite(curvature, residual_gram)
        solution = solution + mix_rows(step_size, direction)
        residual = residual - mix_rows(step_size, applied)
        next_gram = total_squares(residual)
        if iteration + 1 < ITERS:
            direction = residual + mix_rows(solve_definite(residual_gram, next_gram), direction)
        residual_gram = next_gram
    head_table = jnp.transpose(solution, (1, 0, 2)).reshape(test_count, -1)
    ordered = jnp.take(head_table, tile_order[0], axis=1).reshape(test_count, groups, -1)
    arrived = lax.all_to_all(ordered, "dom", split_axis=1, concat_axis=1, tiled=True).reshape(
        test_count, -1
    )
    sensitivity = lax.dot_general(
        kriging.astype(jnp.float32), arrived, (((1,), (1,)), ((), ())), precision=PRECISE
    )
    cell_total = blocks * width_block * groups * lax.axis_size("tile")
    return (sensitivity, residual_gram / cell_total)


def solution(mesh):
    in_specs = (
        P(("dom", "tile"), None),
        P(("dom", "tile"), None),
        P(("dom", "tile"), None),
        P(("dom", "tile"), None),
        P(("dom", "tile"), None),
    )
    out_specs = (P(("dom", "tile"), None), P())
    return jax.shard_map(shards, mesh=mesh, in_specs=in_specs, out_specs=out_specs, check_vma=False)
```

profile of v0, /device:TPU:1, one launch (start us, length us, event | category | flops | bytes accessed | tf_op | source)
XLA Modules:
  0.0 525.7 jit_solution(12580467156202745954)
XLA Ops:
  0.7 1.2 reshape.93
  2.9 4.9 collective-permute-start
  7.9 5.1 collective-permute-start.1
  15.3 1.3 collective-permute-start.3
  16.6 4.0 collective-permute-start.2
  21.2 1.9 collective-permute-done.3
  23.1 1.4 collective-permute-done.2
  26.0 1.0 convolution_add_fusion.1
  27.6 109.2 %all-reduce = (f32[64,64]{1,0:T(8,128)S(1)}, f32[64,64]{1,0:T(8,128)S(1)}) all-reduce(f32[64,64]{1,0:T(8,128)S(1)} %convolution_bitcast_fusion.9, f32[64,64]{1,0:T(8,128)S(1)} %convolution_bitcast_fusion.10), channel_id=1, replica_groups=mesh['dom'=128,'tile'=4] {'dom','tile'}, use_global_device_ids=true, to_apply=%region_3.0 | all-reduce | flops 8192 | bytes 65536 | tf_op jit(solution)/shard_map/psum | solution.py:46
  137.0 5.8 %cholesky.59 = f32[64,64]{1,0:T(8,128)S(1)} custom-call(f32[64,64]{1,0:T(8,128)S(1)} %fusion.24), custom_call_target="Cholesky" | custom-call | tf_op jit(solution)/shard_map/jit(cholesky)/cholesky | solution.py:38
  144.2 4.9 custom-call.13
  150.3 5.8 %cholesky.70 = f32[64,64]{1,0:T(8,128)S(1)} custom-call(f32[64,64]{1,0:T(8,128)S(1)} %fusion.19), custom_call_target="Cholesky" | custom-call | tf_op jit(solution)/shard_map/jit(cholesky)/cholesky | solution.py:38
  157.5 4.9 custom-call.15
  162.9 99.0 %psum.37 = f32[64,64]{1,0:T(8,128)S(1)} all-reduce(f32[64,64]{1,0:T(8,128)S(1)} %convolution_bitcast_fusion.7), channel_id=1, replica_groups=mesh['dom'=128,'tile'=4] {'dom','tile'}, use_global_device_ids=true, to_apply=%region_4.8 | all-reduce | flops 4096 | bytes 32768 | tf_op jit(solution)/shard_map/psum | solution.py:46
  263.8 4.2 collective-permute-start.4
  268.4 1.9 collective-permute-start.5
  270.5 3.0 collective-permute-done.5
  273.5 1.0 fusion.34
  274.6 1.3 collective-permute-start.7
  275.9 4.7 collective-permute-start.6
  281.4 1.5 collective-permute-done.6
  282.9 1.5 maximum_convert_fusion.1
  285.1 1.0 convolution_add_fusion
  286.7 101.5 %psum.38 = f32[64,64]{1,0:T(8,128)S(1)} all-reduce(f32[64,64]{1,0:T(8,128)S(1)} %convolution_bitcast_fusion.5), channel_id=1, replica_groups=mesh['dom'=128,'tile'=4] {'dom','tile'}, use_global_device_ids=true, to_apply=%region_5.9 | all-reduce | flops 4096 | bytes 32768 | tf_op jit(solution)/shard_map/psum | solution.py:74
  388.4 5.8 %cholesky.81 = f32[64,64]{1,0:T(8,128)S(1)} custom-call(f32[64,64]{1,0:T(8,128)S(1)} %fusion.13), custom_call_target="Cholesky" | custom-call | tf_op jit(solution)/shard_map/jit(cholesky)/cholesky | solution.py:38
  395.6 4.9 custom-call.17
  401.7 2.8 gather_fusion
  404.8 1.0 reshape.146
  405.8 10.6 %all-to-all-start = ((f32[128,1,512]{2,1,0:T(1,128)}), f32[128,1,512]{2,1,0:T(1,128)S(1)}, u32[]{:S(2)}, u32[]{:S(2)}) async-start(f32[128,1,512]{2,1,0:T(1,128)} %reshape.146), calls=%async_computation | async-start | bytes 524288 | tf_op jit(solution)/shard_map/all_to_all | solution.py:84
  417.6 104.6 %psum.39 = f32[64,64]{1,0:T(8,128)S(1)} all-reduce(f32[64,64]{1,0:T(8,128)S(1)} %convolution_bitcast_fusion.3), channel_id=1, replica_groups=mesh['dom'=128,'tile'=4] {'dom','tile'}, use_global_device_ids=true, to_apply=%region_6.10 | all-reduce | flops 4096 | bytes 32768 | tf_op jit(solution)/shard_map/psum | solution.py:46
  523.4 1.3 reduce.8
  524.8 0.9 convolution_bitcast_fusion.11
  (87 shorter events, 20.4 us)
Async XLA Ops:
  0.6 524.2 %copy-start = (bf16[16,1024]{1,0:T(8,128)(2,1)S(1)}, bf16[16,1024]{1,0:T(8,128)(2,1)}, u32[]{:S(2)}) copy-start(bf16[16,1024]{1,0:T(8,128)(2,1)} %param.14) | copy-start | bytes 98308
  0.6 1.2 copy-start.1
  2.9 12.0 %collective-permute-start = (bf16[1,2,4096]{2,1,0:T(2,128)(2,1)S(1)}, bf16[1,2,4096]{2,1,0:T(2,128)(2,1)S(1)}, u32[]{:S(2)}, u32[]{:S(2)}) collective-permute-start(bf16[1,2,4096]{2,1,0:T(2,128)(2,1)S(1)} %slice.69), channel_id=1, source_target_pairs={{0,4},{4,8},{8,12},{12,16},{16,20},{20,24},{24,28},{28,32},{32,36}... | collective-permute-start | bytes 49160 | tf_op jit(solution)/shard_map/ppermute | solution.py:19
  7.8 5.8 %copy-start.3 = (s32[1,1024]{1,0:T(1,128)S(1)}, s32[1,1024]{1,0:T(1,128)}, u32[]{:S(2)}) copy-start(s32[1,1024]{1,0:T(1,128)} %param.13) | copy-start | bytes 12292
  7.9 7.1 %collective-permute-start.1 = (bf16[1,2,4096]{2,1,0:T(2,128)(2,1)S(1)}, bf16[1,2,4096]{2,1,0:T(2,128)(2,1)S(1)}, u32[]{:S(2)}, u32[]{:S(2)}) collective-permute-start(bf16[1,2,4096]{2,1,0:T(2,128)(2,1)S(1)} %slice.71), channel_id=1, source_target_pairs={{4,0},{8,4},{12,8},{16,12},{20,16},{24,20},{28,24},{32,28},{36,32}... | collective-permute-start | bytes 49160 | tf_op jit(solution)/shard_map/ppermute | solution.py:20
  15.3 7.8 %collective-permute-start.3 = (bf16[10,1,4096]{2,1,0:T(2,128)(2,1)S(1)}, bf16[10,1,4096]{2,1,0:T(2,128)(2,1)S(1)}, u32[]{:S(2)}, u32[]{:S(2)}) collective-permute-start(bf16[10,1,4096]{2,1,0:T(2,128)(2,1)S(1)} %get-tuple-element.18), channel_id=1, source_target_pairs={{1,0},{2,1},{3,2},{5,4},{6,5},{7,6},{9,8},{10,9},{11,10},{13,12},{... | collective-permute-start | bytes 245768 | tf_op jit(solution)/shard_map/ppermute | solution.py:20
  16.6 7.9 %collective-permute-start.2 = (bf16[10,1,4096]{2,1,0:T(2,128)(2,1)S(1)}, bf16[10,1,4096]{2,1,0:T(2,128)(2,1)S(1)}, u32[]{:S(2)}, u32[]{:S(2)}) collective-permute-start(bf16[10,1,4096]{2,1,0:T(2,128)(2,1)S(1)} %get-tuple-element.17), channel_id=1, source_target_pairs={{0,1},{1,2},{2,3},{4,5},{5,6},{6,7},{8,9},{9,10},{10,11},{12,13},{... | collective-permute-start | bytes 245768 | tf_op jit(solution)/shard_map/ppermute | solution.py:19
  25.3 0.7 copy-start.2
  263.8 6.5 %collective-permute-start.4 = (bf16[1,2,4096]{2,1,0:T(2,128)(2,1)S(1)}, bf16[1,2,4096]{2,1,0:T(2,128)(2,1)S(1)}, u32[]{:S(2)}, u32[]{:S(2)}) collective-permute-start(bf16[1,2,4096]{2,1,0:T(2,128)(2,1)S(1)} %slice.79), channel_id=1, source_target_pairs={{0,4},{4,8},{8,12},{12,16},{16,20},{20,24},{24,28},{28,32},{32,36}... | collective-permute-start | bytes 49160 | tf_op jit(solution)/shard_map/ppermute | solution.py:19
  268.4 5.1 collective-permute-start.5
  274.6 6.8 %collective-permute-start.7 = (bf16[10,1,4096]{2,1,0:T(2,128)(2,1)}, bf16[10,1,4096]{2,1,0:T(2,128)(2,1)}, u32[]{:S(2)}, u32[]{:S(2)}) collective-permute-start(bf16[10,1,4096]{2,1,0:T(2,128)(2,1)} %get-tuple-element.16), channel_id=1, source_target_pairs={{1,0},{2,1},{3,2},{5,4},{6,5},{7,6},{9,8},{10,9},{11,10},{13,12},{... | collective-permute-start | bytes 245768 | tf_op jit(solution)/shard_map/ppermute | solution.py:20
  275.9 7.1 %collective-permute-start.6 = (bf16[10,1,4096]{2,1,0:T(2,128)(2,1)}, bf16[10,1,4096]{2,1,0:T(2,128)(2,1)}, u32[]{:S(2)}, u32[]{:S(2)}) collective-permute-start(bf16[10,1,4096]{2,1,0:T(2,128)(2,1)} %get-tuple-element.15), channel_id=1, source_target_pairs={{0,1},{1,2},{2,3},{4,5},{5,6},{6,7},{8,9},{9,10},{10,11},{12,13},{... | collective-permute-start | bytes 245768 | tf_op jit(solution)/shard_map/ppermute | solution.py:19
  405.8 117.1 %all-to-all-start = ((f32[128,1,512]{2,1,0:T(1,128)}), f32[128,1,512]{2,1,0:T(1,128)S(1)}, u32[]{:S(2)}, u32[]{:S(2)}) async-start(f32[128,1,512]{2,1,0:T(1,128)} %reshape.146), calls=%async_computation | async-start | bytes 524288 | tf_op jit(solution)/shard_map/all_to_all | solution.py:84
where the time goes:
time: 527 us; the launch traced here: 526 us
  blocking collectives  414 us (79%)
  other arithmetic  41.7 us (8%)
  starting transfers between devices  38.1 us (7%)
  local copies, waits for them, and re-layouts  11.3 us (2%)
  matrix products  11.3 us (2%)
  waiting for transfers between devices  7.81 us (1%)
    psum x3, blocking collectives, total_squares(): return symmetric(lax.psum(gram_matrix(residual, residual), ('dom', 'tile')))  313 us
    psum x1, blocking collectives, shards(): lax.psum(gram_matrix(direction, applied), ('dom', 'tile'))  102 us
    another operation x9, other arithmetic, solve_definite(): factor = jnp.linalg.cholesky(matrix)  19.6 us
    ppermute x4, starting transfers between devices, padded_2(): before = lax.ppermute(last, axis, up)  17.8 us
    another operation x6, other arithmetic, solve_definite(): lax.linalg.triangular_solve(factor, lower_part, left_side=True, lower=Tru...  16.6 us
    all_to_all x1, starting transfers between devices, shards(): lax.all_to_all(ordered, 'dom', split_axis=1, concat_axis=1, tiled=True)  10.6 us
  transfers between devices with their start and end apart: 9, of which 4 were waited for; matrix products, arithmetic and copies ran while one was open for 1% of the time, Pallas kernels for 0%

commit v1 on v0

--- a/solution.py
+++ b/solution.py
@@ -43,7 +43,7 @@
 
 
 def total_squares(residual):
-    return symmetric(lax.psum(gram_matrix(residual, residual), ("dom", "tile")))
+    return symmetric(lax.psum(lax.psum(gram_matrix(residual, residual), "dom"), "tile"))
 
 
 def apply_operator(values, matrices, capacity):

time: 527 us -> 1830 us (3.47)
  blocking collectives: 414 us -> 1720 us
    psum x3 -> x6, blocking collectives: 313 us -> 1510 us  [the longest x3 1470 us: total_squares(): lax.psum(gram_matrix(residual, residual), 'dom')]
    psum x1 -> x2, blocking collectives: 102 us -> 208 us  [shards(): lax.psum(gram_matrix(direction, applied), ('dom', 'tile'))]
  transfers between devices with their start and end apart: 9 -> 9, of which waited for: 4 -> 3; matrix products, arithmetic and copies ran while one was open for 1% -> 1% of each run, Pallas kernels for 0% -> 0%
where the time goes in v1:
time: 1830 us
  blocking collectives  1720 us (94%)
  other arithmetic  41.7 us (2%)
  starting transfers between devices  40.7 us (2%)
    psum x3, blocking collectives, total_squares(): lax.psum(gram_matrix(residual, residual), 'dom')  1470 us
    psum x2, blocking collectives, shards(): lax.psum(gram_matrix(direction, applied), ('dom', 'tile'))  208 us
  transfers between devices with their start and end apart: 9, of which 3 were waited for; matrix products, arithmetic and copies ran while one was open for 1% of the time, Pallas kernels for 0%

profile of v1, /device:TPU:1, one launch (start us, length us, event | category | flops | bytes accessed | tf_op | source)
XLA Modules:
  0.0 1826.7 jit_solution(206371884110505244)
XLA Ops:
  0.7 1.2 reshape.93
  2.9 4.9 collective-permute-start
  7.9 5.1 collective-permute-start.1
  13.6 492.2 %psum.57 = f32[64,64]{1,0:T(8,128)S(1)} all-reduce(f32[64,64]{1,0:T(8,128)S(1)} %convolution_bitcast_fusion.9), channel_id=1, replica_groups=mesh['dom'=128,'tile'=4] {'dom'}, use_global_device_ids=true, to_apply=%region_3.0 | all-reduce | flops 4096 | bytes 32768 | tf_op jit(solution)/shard_map/psum | solution.py:46
  505.8 13.7 psum.58
  519.8 5.8 cholesky.70
  529.0 1.3 collective-permute-start.3
  530.3 4.0 collective-permute-start.2
  534.6 4.9 custom-call.15
  541.1 1.0 convolution_add_fusion.1
  542.6 106.6 %psum.56 = f32[64,64]{1,0:T(8,128)S(1)} all-reduce(f32[64,64]{1,0:T(8,128)S(1)} %convolution_bitcast_fusion.10), channel_id=1, replica_groups=mesh['dom'=128,'tile'=4] {'dom','tile'}, use_global_device_ids=true, to_apply=%region_0.0 | all-reduce | flops 4096 | bytes 32768 | tf_op jit(solution)/shard_map/psum | solution.py:74
  649.4 5.8 cholesky.59
  656.6 4.9 custom-call.13
  663.1 489.6 %psum.59 = f32[64,64]{1,0:T(8,128)S(1)} all-reduce(f32[64,64]{1,0:T(8,128)S(1)} %convolution_bitcast_fusion.7), channel_id=1, replica_groups=mesh['dom'=128,'tile'=4] {'dom'}, use_global_device_ids=true, to_apply=%region_5.9 | all-reduce | flops 4096 | bytes 32768 | tf_op jit(solution)/shard_map/psum | solution.py:46
  1152.7 10.9 psum.60
  1165.6 7.1 collective-permute-start.4
  1173.1 5.2 collective-permute-start.5
  1179.1 1.0 fusion.34
  1180.2 1.3 collective-permute-start.7
  1181.5 4.7 collective-permute-start.6
  1188.7 1.5 maximum_convert_fusion.1
  1190.8 1.0 convolution_add_fusion
  1192.4 101.2 %psum.61 = f32[64,64]{1,0:T(8,128)S(1)} all-reduce(f32[64,64]{1,0:T(8,128)S(1)} %convolution_bitcast_fusion.5), channel_id=1, replica_groups=mesh['dom'=128,'tile'=4] {'dom','tile'}, use_global_device_ids=true, to_apply=%region_7.11 | all-reduce | flops 4096 | bytes 32768 | tf_op jit(solution)/shard_map/psum | solution.py:74
  1293.7 5.8 cholesky.81
  1300.9 4.9 custom-call.17
  1307.1 2.8 gather_fusion
  1310.1 1.0 reshape.146
  1311.1 7.1 all-to-all-start
  1319.5 492.1 %psum.62 = f32[64,64]{1,0:T(8,128)S(1)} all-reduce(f32[64,64]{1,0:T(8,128)S(1)} %convolution_bitcast_fusion.3), channel_id=1, replica_groups=mesh['dom'=128,'tile'=4] {'dom'}, use_global_device_ids=true, to_apply=%region_8.12 | all-reduce | flops 4096 | bytes 32768 | tf_op jit(solution)/shard_map/psum | solution.py:46
  1811.5 11.6 psum.63
  1824.3 1.3 reduce.8
  1825.8 0.9 convolution_bitcast_fusion.11
  (92 shorter events, 22.8 us)
Async XLA Ops:
  0.6 1825.1 %copy-start = (bf16[16,1024]{1,0:T(8,128)(2,1)S(1)}, bf16[16,1024]{1,0:T(8,128)(2,1)}, u32[]{:S(2)}) copy-start(bf16[16,1024]{1,0:T(8,128)(2,1)} %param.14) | copy-start | bytes 98308
  0.6 1.2 copy-start.1
  2.9 525.7 %collective-permute-start = (bf16[1,2,4096]{2,1,0:T(2,128)(2,1)S(1)}, bf16[1,2,4096]{2,1,0:T(2,128)(2,1)S(1)}, u32[]{:S(2)}, u32[]{:S(2)}) collective-permute-start(bf16[1,2,4096]{2,1,0:T(2,128)(2,1)S(1)} %slice.69), channel_id=1, source_target_pairs={{0,4},{4,8},{8,12},{12,16},{16,20},{20,24},{24,28},{28,32},{32,36}... | collective-permute-start | bytes 49160 | tf_op jit(solution)/shard_map/ppermute | solution.py:19
  7.9 520.8 %collective-permute-start.1 = (bf16[1,2,4096]{2,1,0:T(2,128)(2,1)S(1)}, bf16[1,2,4096]{2,1,0:T(2,128)(2,1)S(1)}, u32[]{:S(2)}, u32[]{:S(2)}) collective-permute-start(bf16[1,2,4096]{2,1,0:T(2,128)(2,1)S(1)} %slice.71), channel_id=1, source_target_pairs={{4,0},{8,4},{12,8},{16,12},{20,16},{24,20},{28,24},{32,28},{36,32}... | collective-permute-start | bytes 49160 | tf_op jit(solution)/shard_map/ppermute | solution.py:20
  525.6 1.2 copy-start.3
  529.0 10.5 collective-permute-start.3
  530.3 9.2 collective-permute-start.2
  540.4 0.7 copy-start.2
  1165.6 12.7 collective-permute-start.4
  1173.1 6.1 collective-permute-start.5
  1180.2 7.6 collective-permute-start.7
  1181.5 7.2 collective-permute-start.6
  1311.1 512.7 %all-to-all-start = ((f32[128,1,512]{2,1,0:T(1,128)}), f32[128,1,512]{2,1,0:T(1,128)S(1)}, u32[]{:S(2)}, u32[]{:S(2)}) async-start(f32[128,1,512]{2,1,0:T(1,128)} %reshape.146), calls=%async_computation | async-start | bytes 524288 | tf_op jit(solution)/shard_map/all_to_all | solution.py:84
